TPU v7x, 512 devices: a whole 4x8x8 slice. The times are simulated.
512 devices in a mesh: clip: 128 (over z, x_hi, y), space: 4 (over x_lo, core).
Axes of the slice: x: 4 (x_hi: 2, x_lo: 2; x = x_hi * 2 + x_lo), y: 8, z: 8, core: 2. Of those that a mesh axis runs over, the one named last changes fastest.
Arguments:
- tokens: bfloat16 [2048, 96, 1280], P('clip', 'space'), may hold values from -8 to 8, as said below
- w_query: bfloat16 [1280, 640], P('space'), may hold values from -0.4472136 to 0.4472136
- w_key: bfloat16 [1280, 640], P('space'), may hold values from -0.4472136 to 0.4472136
- w_value: bfloat16 [1280, 640], P('space'), may hold values from -0.15625 to 0.15625
- w_out: bfloat16 [640, 1280], P('space'), may hold values from -0.25 to 0.25
- halo_width: int32 [128], P('clip'), may hold values from 1 to 4, as said below
- global_frame: int32 [128], P('clip'), may hold values from 0 to 15
Outputs:
- attended_out: bfloat16 [2048, 96, 1280], P('clip', 'space')
Inputs may be any that keep to these rules, and one draw needn't show every extreme that they name: tokens of order one. `halo_width`: some clip has exactly 4.
All inputs are finite; a program needn't handle non-finite values.
Results may differ from a plain program's by a relative error of at most 0.0075.
Values may be sent and summed in bfloat16 or wider, within the bound.
A program may use at most 64 MiB of HBM per device.

v0:
```python
import math

import jax
import jax.numpy as jnp
from jax import lax
from jax.sharding import PartitionSpec as P

HDIM = 64
HALO = 4


def extended(block, sides, width):
    for axis, dim in sides:
        count = lax.axis_size(axis)
        forward = [(i, i + 1) for i in range(count - 1)]
        backward = [(target, source) for source, target in forward]
        low = lax.ppermute(
            lax.slice_in_dim(block, block.shape[dim] - width, None, axis=dim), axis, forward
        )
        high = lax.ppermute(lax.slice_in_dim(block, 0, width, axis=dim), axis, backward)
        block = jnp.concatenate([low, block, high], axis=dim)
    return block


def add_rows(source, portion):
    return jnp.dot(source, portion, preferred_element_type=jnp.float32)


def body(tokens, w_query, w_key, w_value, w_out, halo_width, global_frame):
    frame_count, place_count, model_width = tokens.shape
    inner_width = w_query.shape[1]
    head_count = inner_width // HDIM
    flat_rows = tokens.reshape(frame_count * place_count, model_width)

    def add_single(portion):
        return add_rows(flat_rows, portion)

    query_sum = add_single(lax.all_gather(w_query, "space", axis=0, tiled=True))
    key_sum = add_single(lax.all_gather(w_key, "space", axis=0, tiled=True))
    value_sum = add_single(lax.all_gather(w_value, "space", axis=0, tiled=True))
    queries = query_sum.astype(jnp.bfloat16).reshape(frame_count, place_count, head_count, HDIM)
    paired = jnp.concatenate([key_sum.astype(jnp.bfloat16), value_sum.astype(jnp.bfloat16)], axis=1)
    paired = paired.reshape(frame_count, place_count, 2 * inner_width)
    near_frames = extended(paired, (("clip", 0),), HALO)
    key_span = near_frames.shape[0]
    near_keys = near_frames[:, :, :inner_width].reshape(key_span, place_count, head_count, HDIM)
    near_values = near_frames[:, :, inner_width:].reshape(key_span, place_count, head_count, HDIM)
    own_frame = lax.dynamic_slice_in_dim(paired, global_frame[0], 1, 0)
    score_scale = 1.0 / math.sqrt(HDIM)
    near_scores = (
        jnp.einsum("fphd,gphd->phfg", queries, near_keys, preferred_element_type=jnp.float32)
        * score_scale
    )
    pool_frames = lax.all_gather(own_frame, "clip", axis=0, tiled=True)
    pool_count = pool_frames.shape[0]
    pool_keys = pool_frames[:, :, :inner_width].reshape(pool_count, place_count, head_count, HDIM)
    pool_values = pool_frames[:, :, inner_width:].reshape(pool_count, place_count, head_count, HDIM)
    far_scores = (
        jnp.einsum("fphd,gphd->phfg", queries, pool_keys, preferred_element_type=jnp.float32)
        * score_scale
    )
    clip_index = lax.axis_index("clip")
    clip_count = lax.axis_size("clip")
    reach_width = halo_width[0]
    key_slot = jnp.arange(key_span)
    before_mask = (key_slot < HALO) & (clip_index > 0) & (HALO - key_slot <= reach_width)
    after_mask = (
        (key_slot >= frame_count + HALO)
        & (clip_index < clip_count - 1)
        & (key_slot - frame_count - HALO + 1 <= reach_width)
    )
    inside_mask = (key_slot >= HALO) & (key_slot < frame_count + HALO)
    valid_key = before_mask | after_mask | inside_mask
    near_scores = jnp.where(valid_key, near_scores, -1e30)
    row_top = jnp.maximum(
        jnp.max(near_scores, axis=-1, keepdims=True), jnp.max(far_scores, axis=-1, keepdims=True)
    )
    near_expos = jnp.where(valid_key, jnp.exp(near_scores - row_top), 0.0)
    far_expos = jnp.exp(far_scores - row_top)
    expo_total = jnp.sum(near_expos, axis=-1, keepdims=True) + jnp.sum(
        far_expos, axis=-1, keepdims=True
    )
    near_weights = (near_expos / expo_total).astype(jnp.bfloat16)
    far_weights = (far_expos / expo_total).astype(jnp.bfloat16)
    mixed = jnp.einsum(
        "phfg,gphd->fphd", near_weights, near_values, preferred_element_type=jnp.float32
    )
    mixed = mixed + jnp.einsum(
        "phfg,gphd->fphd", far_weights, pool_values, preferred_element_type=jnp.float32
    )
    attended = mixed.astype(jnp.bfloat16).reshape(frame_count * place_count, inner_width)
    result = add_rows(attended, lax.all_gather(w_out, "space", axis=0, tiled=True))
    return result.astype(jnp.bfloat16).reshape(frame_count, place_count, model_width)


def solution(mesh):
    return jax.shard_map(
        body,
        mesh=mesh,
        in_specs=(
            P("clip", "space", None),
            P("space", None),
            P("space", None),
            P("space", None),
            P("space", None),
            P("clip"),
            P("clip"),
        ),
        out_specs=P("clip", "space", None),
        check_vma=False,
    )
```

profile of v0, /device:TPU:1, one launch (start us, length us, event | category | flops | bytes accessed | tf_op | source)
XLA Modules:
  0.0 313.1 jit_solution(3726619039046915216)
XLA Ops:
  6.5 0.7 all-gather.6.cloned.1.call-update
  7.3 0.7 all-gather.8.cloned.1.call-update
  8.1 0.7 all-gather.10.cloned.1.call-update
  9.4 36.6 %all-gather.6.cloned.1.call-done = bf16[1280,640]{1,0:T(8,128)(2,1)} async-done(((bf16[320,640]{1,0:T(8,128)(2,1)}), bf16[1280,640]{1,0:T(8,128)(2,1)}) %all-gather.6.cloned.1.call-update) | async-done | bytes 1638416 | tf_op jit(solution)/shard_map/all_gather | solution.py:39
  46.1 2.4 convolution_convert_fusion.3
  48.4 31.4 %all-gather.8.cloned.1.call-done = bf16[1280,640]{1,0:T(8,128)(2,1)} async-done(((bf16[320,640]{1,0:T(8,128)(2,1)}), bf16[1280,640]{1,0:T(8,128)(2,1)}) %all-gather.8.cloned.1.call-update) | async-done | bytes 1638416 | tf_op jit(solution)/shard_map/all_gather | solution.py:40
  79.8 2.4 convolution_convert_fusion.2
  82.3 0.6 constant_dynamic-slice_fusion
  83.0 0.5 all-gather.14.cloned.1.call-update
  84.2 0.8 fusion.20
  85.1 1.3 collective-permute-start.1
  86.3 4.7 %collective-permute-start = (bf16[4,24,1280]{2,1,0:T(8,128)(2,1)}, bf16[4,24,1280]{2,1,0:T(8,128)(2,1)}, u32[]{:S(2)}, u32[]{:S(2)}) collective-permute-start(bf16[4,24,1280]{2,1,0:T(8,128)(2,1)} %bitcast.1), channel_id=1, source_target_pairs={{0,4},{4,8},{8,12},{12,16},{16,20},{20,24},{24,28},{28,32},{32,36}... | collective-permute-start | bytes 737288 | tf_op jit(solution)/shard_map/ppermute | solution.py:17
  91.0 25.6 %all-gather.10.cloned.1.call-done = bf16[1280,640]{1,0:T(8,128)(2,1)} async-done(((bf16[320,640]{1,0:T(8,128)(2,1)}), bf16[1280,640]{1,0:T(8,128)(2,1)}) %all-gather.10.cloned.1.call-update) | async-done | bytes 1638416 | tf_op jit(solution)/shard_map/all_gather | solution.py:38
  116.6 3.1 %convolution_convert_fusion.1 = bf16[384,640]{1,0:T(8,128)(2,1)} fusion(bf16[384,1280]{1,0:T(8,128)(2,1)S(1)} %bitcast.27, bf16[1280,640]{1,0:T(8,128)(2,1)} %all-gather.10.cloned.1.call-done), kind=kOutput, calls=%fused_computation.17 | convolution fusion | flops 629391360 | bytes 3112960 | tf_op jit(solution)/shard_map/dot_general | solution.py:26
  119.8 1.9 reshape.44
  121.7 1.2 pad_maximum_fusion
  122.9 1.0 fusion.27
  123.9 3.9 %reshape.45 = bf16[24,24,10,64]{3,2,1,0:T(8,128)(2,1)} reshape(bf16[24,24,640]{2,1,0:T(8,128)(2,1)} %get-tuple-element.7) | data formatting | bytes 1474560 | tf_op jit(solution)/shard_map/reshape | solution.py:46
  127.8 2.3 reshape.43
  130.1 4.7 %fusion = (f32[24,10,16]{2,1,0:T(8,128)S(1)}, f32[24,10,16,24]{3,2,1,0:T(8,128)}) fusion(pred[24]{0:T(512)(128)(4,1)S(1)} %and_or_fusion, bf16[24,24,10,64]{3,2,1,0:T(8,128)(2,1)} %reshape.45, bf16[16,24,10,64]{3,2,1,0:T(8,128)(2,1)S(1)} %reshape.44), kind=kOutput, calls=%fused_computation.8 | convolution fusion | flops 12069120 | bytes 1612824 | tf_op jit(solution)/shard_map/fphd,gphd->phfg/dot_general | solution.py:51
  134.8 137.1 %all-gather.12.cloned.1.call-done = bf16[128,24,1280]{2,1,0:T(8,128)(2,1)} async-done(((bf16[1,24,1280]{2,1,0:T(8,128)(2,1)}), bf16[128,24,1280]{2,1,0:T(8,128)(2,1)}) %all-gather.12.cloned.1.call-update) | async-done | bytes 7864336 | tf_op jit(solution)/shard_map/all_gather | solution.py:54
  271.9 5.5 %fusion.26 = (bf16[128,24,640]{2,1,0:T(8,128)(2,1)}, bf16[128,24,640]{2,1,0:T(8,128)(2,1)}) fusion(bf16[128,24,1280]{2,1,0:T(8,128)(2,1)} %all-gather.12.cloned.1.call-done), kind=kLoop, calls=%fused_computation.45 | loop fusion | bytes 15728640 | tf_op jit(solution)/shard_map/slice | solution.py:57
  277.4 6.7 %copy.24 = bf16[128,24,640]{0,2,1:T(8,128)(2,1)} copy(bf16[128,24,640]{2,1,0:T(8,128)(2,1)} %get-tuple-element.5) | data formatting | bytes 7864320 | tf_op jit(solution)/shard_map/slice | solution.py:57
  284.1 6.7 %copy.21 = bf16[128,24,640]{0,2,1:T(8,128)(2,1)} copy(bf16[128,24,640]{2,1,0:T(8,128)(2,1)} %get-tuple-element.6) | data formatting | bytes 7864320 | tf_op jit(solution)/shard_map/slice | solution.py:56
  290.8 3.4 %multiply_reduce_fusion = (f32[24,10,16]{2,1,0:T(8,128)S(1)}, f32[24,10,16,128]{3,2,1,0:T(8,128)S(1)}) fusion(bf16[128,24,10,64]{0,3,2,1:T(8,128)(2,1)} %bitcast.28, bf16[16,24,10,64]{3,2,1,0:T(8,128)(2,1)S(1)} %reshape.44), kind=kOutput, calls=%fused_computation.7 | convolution fusion | flops 63893760 | bytes 6405120 | tf_op jit(solution)/shard_map/fphd,gphd->phfg/dot_general | solution.py:59
  294.2 1.3 fusion.1
  295.7 1.3 fusion.6
  297.3 1.5 fusion.2
  298.8 0.6 copy-done.1
  299.4 2.6 fusion.7
  302.4 0.8 reshape.48
  303.3 3.3 %convolution_convert_fusion = bf16[384,1280]{1,0:T(8,128)(2,1)} fusion(bf16[384,640]{1,0:T(8,128)(2,1)S(1)} %reshape.48, bf16[640,1280]{1,0:T(8,128)(2,1)} %all-gather.14.cloned.1.call-done), kind=kOutput, calls=%fused_computation | convolution fusion | flops 629637120 | bytes 3112960 | tf_op jit(solution)/shard_map/dot_general | solution.py:26
  (21 shorter events, 1.1 us)
Async XLA Ops:
  6.5 39.5 %copy-start = (bf16[16,24,1280]{2,1,0:T(8,128)(2,1)S(1)}, bf16[16,24,1280]{2,1,0:T(8,128)(2,1)}, u32[]{:S(2)}) copy-start(bf16[16,24,1280]{2,1,0:T(8,128)(2,1)} %param.7) | copy-start | bytes 2949124
  6.5 39.5 %all-gather.6.cloned.1.call-start = ((), (), s32[]{:S(2)}) async-start(), calls=%async_computation | async-start | bytes 2048000 | tf_op jit(solution)/shard_map/all_gather | solution.py:39
  7.3 72.6 %all-gather.8.cloned.1.call-start = ((), (), s32[]{:S(2)}) async-start(), calls=%async_computation.1 | async-start | bytes 2048000 | tf_op jit(solution)/shard_map/all_gather | solution.py:40
  8.0 108.6 %all-gather.10.cloned.1.call-start = ((), (), s32[]{:S(2)}) async-start(), calls=%async_computation.2 | async-start | bytes 2048000 | tf_op jit(solution)/shard_map/all_gather | solution.py:38
  8.7 263.2 %all-gather.12.cloned.1.call-start = ((), (), s32[]{:S(2)}) async-start(), calls=%async_computation.3 | async-start | bytes 7925760 | tf_op jit(solution)/shard_map/all_gather | solution.py:54
  83.0 220.3 %all-gather.14.cloned.1.call-start = ((), (), s32[]{:S(2)}) async-start(), calls=%async_computation.4 | async-start | bytes 2048000 | tf_op jit(solution)/shard_map/all_gather | solution.py:92
  85.1 36.6 %collective-permute-start.1 = (bf16[4,24,1280]{2,1,0:T(8,128)(2,1)}, bf16[4,24,1280]{2,1,0:T(8,128)(2,1)}, u32[]{:S(2)}, u32[]{:S(2)}) collective-permute-start(bf16[4,24,1280]{2,1,0:T(8,128)(2,1)} %bitcast.3), channel_id=1, source_target_pairs={{4,0},{8,4},{12,8},{16,12},{20,16},{24,20},{28,24},{32,28},{36,32}... | collective-permute-start | bytes 737288 | tf_op jit(solution)/shard_map/ppermute | solution.py:20
  86.3 35.3 %collective-permute-start = (bf16[4,24,1280]{2,1,0:T(8,128)(2,1)}, bf16[4,24,1280]{2,1,0:T(8,128)(2,1)}, u32[]{:S(2)}, u32[]{:S(2)}) collective-permute-start(bf16[4,24,1280]{2,1,0:T(8,128)(2,1)} %bitcast.1), channel_id=1, source_target_pairs={{0,4},{4,8},{8,12},{12,16},{16,20},{20,24},{24,28},{28,32},{32,36}... | collective-permute-start | bytes 737288 | tf_op jit(solution)/shard_map/ppermute | solution.py:17
  294.2 1.6 copy-start.3
  295.5 1.8 copy-start.2
  297.3 2.2 copy-start.1
Sparse Core Ops, SparseCore 0:
  9.5 36.5 all-gather.5
  48.2 31.6 all-gather.7
  81.9 34.6 all-gather.9
  120.8 151.0 all-gather.11
  273.9 28.8 all-gather.13
where the time goes:
time: 316 us; the launch traced here: 313 us
  waiting for transfers between devices  233 us (74%)
  local copies, waits for them, and re-layouts  30.8 us (10%)
  matrix products  23.3 us (7%)
  between operations  14.6 us (5%)
  starting transfers between devices  6.13 us (2%)
  other arithmetic  4.81 us (2%)
    all_gather x1, waiting for transfers between devices, body(): pool_frames = lax.all_gather(own_frame, 'clip', axis=0, tiled=True)  137 us
    all_gather x1, waiting for transfers between devices, body(): key_sum = add_single(lax.all_gather(w_key, 'space', axis=0, tiled=True))  36.6 us
    all_gather x1, waiting for transfers between devices, body(): value_sum = add_single(lax.all_gather(w_value, 'space', axis=0, tiled=True))  31.4 us
    all_gather x1, waiting for transfers between devices, body(): query_sum = add_single(lax.all_gather(w_query, 'space', axis=0, tiled=True))  25.6 us
    slice x2, local copies, waits for them, and re-layouts, body(): pool_frames[:, :, inner_width:]  12.2 us
    dot_general x4, matrix products, add_rows(): return jnp.dot(source, portion, preferred_element_type=jnp.float32)  11.2 us
    slice x1, local copies, waits for them, and re-layouts, body(): pool_frames[:, :, :inner_width]  6.68 us
  transfers between devices with their start and end apart: 7, of which 4 were waited for; matrix products, arithmetic and copies ran while one was open for 17% of the time, Pallas kernels for 0%

commit v1 on v0

v1 whole, which is shorter than its diff:
```python
import jax
import jax.numpy as jnp
from jax import lax
from jax.experimental import pallas as pl
from jax.experimental.pallas import tpu as pltpu
from jax.sharding import PartitionSpec as P

MESH = pl.DeviceIdType.MESH
BF = jnp.bfloat16
F32 = jnp.float32

RING = 8
C = 1280
INNER = 640
FRAMES = 16
PLACES = 24
ROWS = FRAMES * PLACES
HALO = 4
PAIRS = 5
SCALE = 0.125
LOW = -1e30
PARTS = ((0, 2), (16, 1))
SPOTS = ((0, 0), (0, 1), (1, 0))
WIDE = INNER + 128


def iota(shape, dim):
    return lax.broadcasted_iota(jnp.int32, shape, dim)


def onehot(mask):
    return jnp.where(mask, 1.0, 0.0).astype(BF)


def dot(a, b):
    return jnp.dot(a, b, preferred_element_type=F32)


def dot_t(a, b):
    return lax.dot_general(a, b, (((1,), (1,)), ((), ())), preferred_element_type=F32)


def kernel(
    tok_hbm, wq_hbm, wk_hbm, wv_hbm, wo_hbm, halo_s, gf_s, out_ref,
    tok, xt, htok, xht, wq, wk, wv, wo, q_own, qz, qy, k_own, v_own, k_mar, v_mar, k_pool, v_pool,
    mz, my, rz, ry, poolz, pooly, obuf, og, near_o, near_l, att,
    loc_sem, w_send, w_recv, h_send, h_recv, m_send, m_recv, r_send, r_recv, q_send, q_recv, o_send, o_recv,
):
    c = lax.axis_index("clip")
    s = lax.axis_index("space")
    z, xh, y = c // 16, (c // 8) % 2, c % 8
    xl, core = s // 2, s % 2
    x = xh * 2 + xl

    def dev(z_, xh_, y_, s_):
        return (z_ * 16 + xh_ * 8 + y_, s_)

    mate = (c, xl * 2 + 1 - core)
    up = (x + 1) % 4
    down = (x + 3) % 4
    x_up = dev(z, up // 2, y, (up % 2) * 2 + core)
    x_down = dev(z, down // 2, y, (down % 2) * 2 + core)
    clip_next = ((c + 1) % 128, s)
    clip_prev = ((c + 127) % 128, s)
    own = (z, y)
    across = (y, z)

    def ring_dev(part, place, xh_):
        return dev(place, xh_, y, s) if part == 0 else dev(z, xh_, place, s)

    def cross_dev(part, place):
        return dev(z, xh, place, s) if part == 0 else dev(place, xh, y, s)

    weights = ((wq_hbm, wq), (wk_hbm, wk), (wv_hbm, wv), (wo_hbm, wo))
    tok_in = pltpu.make_async_copy(tok_hbm, tok, loc_sem.at[0])
    tok_in.start()

    def shard(i, index, half=None):
        full = weights[i][1]
        rows = full.shape[0] // 4
        if half is None:
            return full.at[pl.ds(pl.multiple_of(index * rows, 16), rows)]
        return full.at[pl.ds(pl.multiple_of(index * rows + half * (rows // 2), 16), rows // 2)]

    w_in = []
    for i in range(4):
        copy = pltpu.make_async_copy(weights[i][0], shard(i, s), loc_sem.at[1 + i])
        copy.start()
        w_in.append(copy)

    barrier = pltpu.get_barrier_semaphore()

    def greet(device):
        pl.semaphore_signal(barrier, inc=1, device_id=device, device_id_type=MESH)

    for part in range(2):
        def greet_same(d, carry, part=part):
            greet(ring_dev(part, (own[part] + d) % RING, xh))
            return carry

        def greet_other(d, carry, part=part):
            greet(ring_dev(part, (own[part] + d) % RING, 1 - xh))
            return carry

        lax.fori_loop(1, RING, greet_same, 0)
        lax.fori_loop(0, RING, greet_other, 0)
    for device in (mate, x_up, x_down, clip_next, clip_prev):
        greet(device)

    tok_in.wait()
    frame = gf_s[0]
    pick = onehot(iota((PLACES, ROWS), 1) == iota((PLACES, ROWS), 0) + frame * PLACES)
    picked = dot(pick, tok[...]).astype(BF)
    for part, buf in ((0, mz), (1, my)):
        first, count = PARTS[part]
        shape = (RING * 16, PLACES)
        spot = iota(shape, 1) - first - (iota(shape, 0) >> 4) * count
        row = iota(shape, 0) & 15
        inside = (spot >= 0) & (spot < count)
        total = jnp.zeros((RING * 16, 256), F32)
        for j in range(5):
            choose = onehot(inside & (row == spot * 5 + j))
            total = total + dot(choose, picked[:, 256 * j : 256 * j + 256])
        buf[...] = total.astype(BF).reshape(RING, 16, 256)

    pl.semaphore_wait(barrier, 2 * (2 * RING - 1) + 5)

    def message(part, d, other):
        send, land = ((mz, rz), (my, ry))[part]
        place = (own[part] + d) % RING
        xh_ = 1 - xh if other else xh
        k = d + (RING if other else 0)
        return pltpu.make_async_remote_copy(
            src_ref=send.at[place],
            dst_ref=land.at[xh * RING + own[part]],
            send_sem=m_send.at[part, k],
            recv_sem=m_recv.at[part, k],
            device_id=ring_dev(part, place, xh_),
            device_id_type=MESH,
        )

    def each_message(act):
        for part in range(2):
            def same(d, carry, part=part):
                act(message(part, d, False))
                return carry

            def other(d, carry, part=part):
                act(message(part, d, True))
                return carry

            lax.fori_loop(1, RING, same, 0)
            lax.fori_loop(0, RING, other, 0)

    def weight_copy(i, kind):
        rows = weights[i][0].shape[0]
        theirs = (1 - xl) * 2 + core
        if kind == 0:
            src, dst, device = weights[i][0].at[pl.ds(0, rows // 2)], shard(i, s, 0), x_up
        elif kind == 1:
            src, dst, device = weights[i][0].at[pl.ds(rows // 2, rows // 2)], shard(i, s, 1), x_down
        elif kind == 2:
            src, dst, device = weights[i][0], shard(i, s), mate
        else:
            src, dst, device = shard(i, theirs, kind - 3), shard(i, theirs, kind - 3), mate
        return pltpu.make_async_remote_copy(
            src_ref=src, dst_ref=dst, send_sem=w_send.at[i, kind], recv_sem=w_recv.at[i, kind],
            device_id=device, device_id_type=MESH,
        )

    def margin_copy(side):
        edge = HALO * PLACES
        src = tok_hbm.at[pl.ds(ROWS - edge, edge)] if side == 0 else tok_hbm.at[pl.ds(0, edge)]
        return pltpu.make_async_remote_copy(
            src_ref=src,
            dst_ref=htok.at[pl.ds(side * edge, edge)],
            send_sem=h_send.at[side],
            recv_sem=h_recv.at[side],
            device_id=clip_next if side == 0 else clip_prev,
            device_id_type=MESH,
        )

    each_message(lambda copy: copy.start())
    for kind in range(3):
        weight_copy(0, kind).start()
    for side in range(2):
        margin_copy(side).start()
    for i in range(1, 4):
        for kind in range(3):
            weight_copy(i, kind).start()

    shape = (ROWS, ROWS)
    turn = onehot(iota(shape, 1) == (iota(shape, 0) & 15) * PLACES + (iota(shape, 0) >> 4))
    xt[...] = dot(turn, tok[...]).astype(BF)

    rz[xh * RING + z] = mz[z]
    ry[xh * RING + y] = my[y]
    each_message(lambda copy: copy.wait_recv())
    pools = (poolz, pooly)
    for part, land in ((0, rz), (1, ry)):
        count = PARTS[part][1]
        shape = (count * 16, 256)
        r, col = iota(shape, 0), iota(shape, 1)
        for j in range(5):
            choose = onehot(((r & 15) == (col >> 4)) & ((col & 15) == (r >> 4) * 5 + j))
            block = dot(choose, land[...].reshape(256, 256)).astype(BF)
            pools[part][across[part], :, :, 256 * j : 256 * j + 256] = block.reshape(count, 16, 256)

    def ring_copy(part, way, step):
        b = across[part]
        pool = pools[part]
        if way == 0:
            origin, device = (b + RING - step) % RING, cross_dev(part, (b + 1) % RING)
        else:
            origin, device = (b + step) % RING, cross_dev(part, (b + RING - 1) % RING)
        block = pool.at[origin]
        if step == 3 and part == 0:
            block = pool.at[origin, way]
        return pltpu.make_async_remote_copy(
            src_ref=block, dst_ref=block, send_sem=r_send.at[part, way, step], recv_sem=r_recv.at[part, way, step],
            device_id=device, device_id_type=MESH,
        )

    def ring_pieces(step):
        if step < 3:
            return ((0, 0), (0, 1), (1, 0), (1, 1))
        return ((0, 0), (0, 1), (1, 0))

    def ring_step(step):
        for part, way in ring_pieces(step):
            if step > 0:
                ring_copy(part, way, step - 1).wait_recv()
            ring_copy(part, way, step).start()
        if step == 3:
            ring_copy(1, 1, 2).wait_recv()

    def pass_on(i):
        weight_copy(i, 0).wait_recv()
        weight_copy(i, 3).start()
        weight_copy(i, 1).wait_recv()
        weight_copy(i, 4).start()

    def whole(i):
        w_in[i].wait()
        for kind in range(2, 5):
            weight_copy(i, kind).wait_recv()

    ring_step(0)

    pass_on(0)
    whole(0)
    q_own[...] = (dot(xt[...], wq[...]) * SCALE).astype(BF)

    def query_copy(part, d):
        first, count = PARTS[part]
        place = (own[part] + d) % RING
        rows = count * 16
        return pltpu.make_async_remote_copy(
            src_ref=q_own.at[pl.ds(pl.multiple_of(first * 16 + place * rows, 16), rows)],
            dst_ref=(qz, qy)[part].at[own[part]],
            send_sem=q_send.at[part, d],
            recv_sem=q_recv.at[part, d],
            device_id=ring_dev(part, place, xh),
            device_id_type=MESH,
        )

    def each_query(act):
        for part in range(2):
            def one(d, carry, part=part):
                act(query_copy(part, d))
                return carry

            lax.fori_loop(1, RING, one, 0)

    each_query(lambda copy: copy.start())
    qz[z] = q_own[pl.ds(pl.multiple_of(z * 32, 16), 32)]
    qy[y] = q_own[pl.ds(pl.multiple_of(256 + y * 16, 16), 16)]
    ring_step(1)

    for side in range(2):
        margin_copy(side).wait_recv()
    edge = 2 * HALO * PLACES
    shape = (edge, edge)
    turn = onehot(iota(shape, 1) == (iota(shape, 0) & 7) * PLACES + (iota(shape, 0) >> 3))
    xht[...] = dot(turn, htok[...]).astype(BF)

    ring_step(2)
    pass_on(1)
    whole(1)
    k_own[...] = dot(xt[...], wk[...]).astype(BF)
    k_mar[...] = dot(xht[...], wk[...]).astype(BF)
    ring_step(3)
    pass_on(2)
    for part, way in ring_pieces(3):
        ring_copy(part, way, 3).wait_recv()
    for k, (part, p) in enumerate(SPOTS):
        k_pool[k] = dot(pools[part][:, p].reshape(RING * 16, C), wk[...]).astype(BF)
    whole(2)
    for k, (part, p) in enumerate(SPOTS):
        v_pool[k] = dot(pools[part][:, p].reshape(RING * 16, C), wv[...]).astype(BF)

    each_query(lambda copy: copy.wait_recv())
    lane = iota((128, 128), 1)
    left = lane < 64
    left_b = onehot(iota((1, 128), 1) < 64)
    right_b = onehot(iota((1, 128), 1) >= 64)

    def reply_copy(k, d):
        part, p = SPOTS[k]
        first, count = PARTS[part]
        place = (own[part] + d) % RING
        return pltpu.make_async_remote_copy(
            src_ref=obuf.at[k, place],
            dst_ref=og.at[pl.ds(pl.multiple_of((first + own[part] * count + p) * 16, 16), 16)],
            send_sem=o_send.at[k, d],
            recv_sem=o_recv.at[k, d],
            device_id=ring_dev(part, place, xh),
            device_id_type=MESH,
        )

    def each_reply(k, act):
        def one(d, carry):
            act(reply_copy(k, d))
            return carry

        lax.fori_loop(1, RING, one, 0)

    for k, (part, p) in enumerate(SPOTS):
        first, count = PARTS[part]
        queries = (qz, qy)[part]
        logs = jnp.zeros((128, 128), F32)
        for pair in range(PAIRS):
            lanes = slice(128 * pair, 128 * pair + 128)
            q = queries[:, 16 * p : 16 * p + 16, lanes].reshape(128, 128)
            keys = k_pool[k, :, lanes]
            values = v_pool[k, :, lanes]
            scores = dot_t(q, jnp.concatenate([keys * left_b, keys * right_b], axis=0))
            s0, s1 = scores[:, :128], scores[:, 128:]
            m0 = jnp.max(s0, axis=1, keepdims=True)
            m1 = jnp.max(s1, axis=1, keepdims=True)
            e0 = jnp.exp(s0 - m0)
            e1 = jnp.exp(s1 - m1)
            l0 = jnp.sum(e0, axis=1, keepdims=True)
            l1 = jnp.sum(e1, axis=1, keepdims=True)
            mixed = dot(
                jnp.concatenate([e0.astype(BF), e1.astype(BF)], axis=1),
                jnp.concatenate([values * left_b, values * right_b], axis=0),
            )
            mixed = mixed * jnp.where(left, 1.0 / l0, 1.0 / l1)
            obuf[k, :, :, lanes] = mixed.astype(BF).reshape(RING, 16, 128)
            logs = jnp.where(lane == 2 * pair, m0 + jnp.log(l0), logs)
            logs = jnp.where(lane == 2 * pair + 1, m1 + jnp.log(l1), logs)
        high = logs.astype(BF).astype(F32)
        middle = (logs - high).astype(BF).astype(F32)
        low = (logs - high - middle).astype(BF).astype(F32)
        packed = high + pltpu.roll(middle, 16, 1) + pltpu.roll(low, 32, 1)
        obuf[k, :, :, INNER:] = packed.astype(BF).reshape(RING, 16, 128)
        each_reply(k, lambda copy: copy.start())
        og[pl.ds(pl.multiple_of((first + own[part] * count + p) * 16, 16), 16)] = obuf[k, own[part]]

    pass_on(3)

    v_own[...] = dot(xt[...], wv[...]).astype(BF)
    v_mar[...] = dot(xht[...], wv[...]).astype(BF)
    row8 = iota((128, 128), 0) >> 4
    own_bias = jnp.where(row8 == (lane >> 4), 0.0, LOW)
    half = lane & 63
    slot = half & 7
    reach = halo_s[0]
    before = (slot < HALO) & (c > 0) & (HALO - slot <= reach)
    after = (slot >= HALO) & (c < 127) & (slot - HALO + 1 <= reach)
    mar_bias = jnp.where((row8 == (half >> 3)) & (before | after), 0.0, LOW)
    for g in range(3):
        rows = slice(128 * g, 128 * g + 128)
        edges = slice(64 * g, 64 * g + 64)
        logs = jnp.zeros((128, 128), F32)
        for pair in range(PAIRS):
            lanes = slice(128 * pair, 128 * pair + 128)
            q = q_own[rows, lanes]
            ko, vo, km, vm = k_own[rows, lanes], v_own[rows, lanes], k_mar[edges, lanes], v_mar[edges, lanes]
            scores = dot_t(q, jnp.concatenate([ko * left_b, ko * right_b, km * left_b, km * right_b], axis=0))
            s0 = scores[:, :128] + own_bias
            s1 = scores[:, 128:256] + own_bias
            sm = scores[:, 256:] + mar_bias
            m0 = jnp.max(jnp.maximum(s0, jnp.where(left, sm, LOW)), axis=1, keepdims=True)
            m1 = jnp.max(jnp.maximum(s1, jnp.where(left, LOW, sm)), axis=1, keepdims=True)
            e0 = jnp.exp(s0 - m0)
            e1 = jnp.exp(s1 - m1)
            em = jnp.exp(sm - jnp.where(left, m0, m1))
            l0 = jnp.sum(e0 + jnp.where(left, em, 0.0), axis=1, keepdims=True)
            l1 = jnp.sum(e1 + jnp.where(left, 0.0, em), axis=1, keepdims=True)
            mixed = dot(
                jnp.concatenate([e0.astype(BF), e1.astype(BF), em.astype(BF)], axis=1),
                jnp.concatenate([vo * left_b, vo * right_b, vm * left_b, vm * right_b], axis=0),
            )
            near_o[rows, lanes] = mixed * jnp.where(left, 1.0 / l0, 1.0 / l1)
            logs = jnp.where(lane == 2 * pair, m0 + jnp.log(l0), logs)
            logs = jnp.where(lane == 2 * pair + 1, m1 + jnp.log(l1), logs)
        near_l[rows, :] = logs

    for k in range(3):
        each_reply(k, lambda copy: copy.wait_recv())
    r128, c128 = iota((128, 128), 0), iota((128, 128), 1)
    gather_logs = onehot(((r128 & 15) == c128) & (r128 < 48) & (c128 < 10))
    expand = onehot(iota((128, INNER), 0) == (iota((128, INNER), 1) >> 6))
    for g in range(3):
        rows = slice(128 * g, 128 * g + 128)
        far_l = dot(og[rows, INNER:], gather_logs)
        share = 1.0 / (1.0 + jnp.exp(near_l[rows, :] - far_l))
        high = share.astype(BF)
        rest = (share - high.astype(F32)).astype(BF)
        wide = dot(high, expand) + dot(rest, expand)
        near = near_o[rows, :]
        att[rows, :] = (near + wide * (og[rows, :INNER].astype(F32) - near)).astype(BF)
    shape = (ROWS, ROWS)
    turn = onehot(iota(shape, 0) == (iota(shape, 1) & 15) * PLACES + (iota(shape, 1) >> 4))
    ordered = dot(turn, att[...]).astype(BF)
    whole(3)
    out_ref[...] = dot(ordered, wo[...]).astype(BF)

    each_message(lambda copy: copy.wait_send())
    for i in range(4):
        for kind in range(5):
            weight_copy(i, kind).wait_send()
    for side in range(2):
        margin_copy(side).wait_send()
    for step in range(4):
        for part, way in ring_pieces(step):
            ring_copy(part, way, step).wait_send()
    each_query(lambda copy: copy.wait_send())
    for k in range(3):
        each_reply(k, lambda copy: copy.wait_send())


def body(tokens, w_query, w_key, w_value, w_out, halo_width, global_frame):
    rows = tokens.reshape(ROWS, C)
    any_spec = pl.BlockSpec(memory_space=pl.ANY)
    smem = pl.BlockSpec(memory_space=pltpu.SMEM)
    v = pltpu.VMEM
    dma = pltpu.SemaphoreType.DMA
    edge = 2 * HALO * PLACES
    out = pl.pallas_call(
        kernel,
        out_shape=jax.ShapeDtypeStruct((ROWS, C), BF),
        in_specs=[any_spec] * 5 + [smem] * 2,
        out_specs=pl.BlockSpec(memory_space=pltpu.VMEM),
        scratch_shapes=[
            v((ROWS, C), BF), v((ROWS, C), BF), v((edge, C), BF), v((edge, C), BF),
            v((C, INNER), BF), v((C, INNER), BF), v((C, INNER), BF), v((INNER, C), BF),
            v((ROWS, INNER), BF), v((RING, 32, INNER), BF), v((RING, 16, INNER), BF),
            v((ROWS, INNER), BF), v((ROWS, INNER), BF), v((edge, INNER), BF), v((edge, INNER), BF),
            v((3, 128, INNER), BF), v((3, 128, INNER), BF),
            v((RING, 16, 256), BF), v((RING, 16, 256), BF), v((16, 16, 256), BF), v((16, 16, 256), BF),
            v((RING, 2, 16, C), BF), v((RING, 1, 16, C), BF),
            v((3, RING, 16, WIDE), BF), v((ROWS, WIDE), BF),
            v((ROWS, INNER), F32), v((ROWS, 128), F32), v((ROWS, INNER), BF),
            dma((5,)), dma((4, 5)), dma((4, 5)), dma((2,)), dma((2,)), dma((2, 16)), dma((2, 16)),
            dma((2, 2, 4)), dma((2, 2, 4)), dma((2, 8)), dma((2, 8)), dma((3, 8)), dma((3, 8)),
        ],
        compiler_params=pltpu.CompilerParams(
            collective_id=0, has_side_effects=True, vmem_limit_bytes=48 * 1024 * 1024
        ),
    )(rows, w_query, w_key, w_value, w_out, halo_width, global_frame)
    return out.reshape(FRAMES, PLACES, C)


def solution(mesh):
    return jax.shard_map(
        body,
        mesh=mesh,
        in_specs=(
            P("clip", "space", None),
            P("space", None),
            P("space", None),
            P("space", None),
            P("space", None),
            P("clip"),
            P("clip"),
        ),
        out_specs=P("clip", "space", None),
        check_vma=False,
    )
```

time: 316 us -> 77.5 us (0.25)
  waiting for transfers between devices: 233 us -> 0 us
  Pallas kernels: 0 us -> 69.7 us
  local copies, waits for them, and re-layouts: 30.8 us -> 6.15 us
  matrix products: 23.3 us -> 0 us
  between operations: 14.6 us -> 1.32 us
  starting transfers between devices: 6.13 us -> 0 us
  other arithmetic: 4.81 us -> 0 us
    all_gather x5 -> x0, waiting for transfers between devices: 231 us -> none  [the longest x1 137 us: body(): pool_frames = lax.all_gather(own_frame, 'clip', axis=0, tiled=True)]
    pallas_call x0 -> x1, Pallas kernels: none -> 69.7 us  [body(): pl.pallas_call(kernel, out_shape=jax.ShapeDtypeStruct((ROWS, C), BF), in_...]
    dot_general x8 -> x0, matrix products: 23.3 us -> none  [the longest x4 11.2 us: add_rows(): return jnp.dot(source, portion, preferred_element_type=jnp.float32)]
    slice x4 -> x0, local copies, waits for them, and re-layouts: 19.8 us -> none  [the longest x2 12.2 us: body(): pool_frames[:, :, inner_width:]]
    reshape x4 -> x0, local copies, waits for them, and re-layouts: 8.89 us -> none  [the longest x1 3.9 us: body(): near_frames[:, :, :inner_width]]
    ppermute x2 -> x0, starting transfers between devices: 5.98 us -> none  [the longest x1 4.7 us: extended(): lax.ppermute(lax.slice_in_dim(block, block.shape[dim] - width, None, axis...]
    unnamed x8 -> x11, local copies, waits for them, and re-layouts: 1.06 us -> 6.15 us
  transfers between devices with their start and end apart: 7 -> 0, of which waited for: 4 -> 0; matrix products, arithmetic and copies ran while one was open for 17% -> 0% of each run, Pallas kernels for 0% -> 0%
where the time goes in v1:
time: 77.5 us; the launch traced here: 77.2 us
  Pallas kernels  69.7 us (90%)
  local copies, waits for them, and re-layouts  6.15 us (8%)
  between operations  1.32 us (2%)
    pallas_call x1, Pallas kernels, body(): pl.pallas_call(kernel, out_shape=jax.ShapeDtypeStruct((ROWS, C), BF), in_...  69.7 us
    unnamed x11, local copies, waits for them, and re-layouts  6.15 us

profile of v1, /device:TPU:1, one launch (start us, length us, event | category | flops | bytes accessed | tf_op | source)
XLA Modules:
  0.0 77.2 jit_solution(9914096625752362888)
XLA Ops:
  1.3 0.0 copy-start
  1.3 1.2 %copy-done = bf16[16,24,1280]{2,1,0:T(8,128)(2,1)S(1)} copy-done((bf16[16,24,1280]{2,1,0:T(8,128)(2,1)S(1)}, bf16[16,24,1280]{2,1,0:T(8,128)(2,1)}, u32[]{:S(2)}) %copy-start) | copy-done | bytes 983064
  2.5 0.0 copy-start.1
  2.5 1.0 %copy-done.1 = bf16[320,640]{1,0:T(8,128)(2,1)S(1)} copy-done((bf16[320,640]{1,0:T(8,128)(2,1)S(1)}, bf16[320,640]{1,0:T(8,128)(2,1)}, u32[]{:S(2)}) %copy-start.1) | copy-done | bytes 409624
  3.5 0.0 copy-start.2
  3.5 1.0 %copy-done.2 = bf16[320,640]{1,0:T(8,128)(2,1)S(1)} copy-done((bf16[320,640]{1,0:T(8,128)(2,1)S(1)}, bf16[320,640]{1,0:T(8,128)(2,1)}, u32[]{:S(2)}) %copy-start.2) | copy-done | bytes 409624
  4.5 0.0 copy-start.3
  4.5 1.0 %copy-done.3 = bf16[320,640]{1,0:T(8,128)(2,1)S(1)} copy-done((bf16[320,640]{1,0:T(8,128)(2,1)S(1)}, bf16[320,640]{1,0:T(8,128)(2,1)}, u32[]{:S(2)}) %copy-start.3) | copy-done | bytes 409624
  5.5 0.0 copy-start.4
  5.5 1.0 %copy-done.4 = bf16[160,1280]{1,0:T(8,128)(2,1)S(1)} copy-done((bf16[160,1280]{1,0:T(8,128)(2,1)S(1)}, bf16[160,1280]{1,0:T(8,128)(2,1)}, u32[]{:S(2)}) %copy-start.4) | copy-done | bytes 409624
  6.5 69.7 %shard_map.73 = bf16[384,1280]{1,0:T(8,128)(2,1)S(1)} custom-call(bf16[384,1280]{1,0:T(8,128)(2,1)S(1)} %bitcast.3, bf16[320,640]{1,0:T(8,128)(2,1)S(1)} %copy-done.1, bf16[320,640]{1,0:T(8,128)(2,1)S(1)} %copy-done.2, bf16[320,640]{1,0:T(8,128)(2,1)S(1)} %copy-done.3, bf16[160,1280]{1,0:T(8,128)(2,1)S(1)} %copy-done.4, s32[1]{0:T(128)S(6)} %copy.9.halo_s, ...), custom_call_target="tpu_custom_call" | custom-call | tf_op jit(solution)/shard_map/pallas_call | solution.py:442
  76.2 0.9 %copy.11 = bf16[16,24,1280]{2,1,0:T(8,128)(2,1)} copy(bf16[16,24,1280]{2,1,0:T(8,128)(2,1)S(1)} %bitcast.2) | data formatting | bytes 1966080
Async XLA Ops:
  1.3 1.2 %copy-start = (bf16[16,24,1280]{2,1,0:T(8,128)(2,1)S(1)}, bf16[16,24,1280]{2,1,0:T(8,128)(2,1)}, u32[]{:S(2)}) copy-start(bf16[16,24,1280]{2,1,0:T(8,128)(2,1)} %param.7) | copy-start | bytes 2949124
  2.5 1.0 %copy-start.1 = (bf16[320,640]{1,0:T(8,128)(2,1)S(1)}, bf16[320,640]{1,0:T(8,128)(2,1)}, u32[]{:S(2)}) copy-start(bf16[320,640]{1,0:T(8,128)(2,1)} %wq_hbm.1) | copy-start | bytes 1228804
  3.5 1.0 %copy-start.2 = (bf16[320,640]{1,0:T(8,128)(2,1)S(1)}, bf16[320,640]{1,0:T(8,128)(2,1)}, u32[]{:S(2)}) copy-start(bf16[320,640]{1,0:T(8,128)(2,1)} %wk_hbm.1) | copy-start | bytes 1228804
  4.5 1.0 %copy-start.3 = (bf16[320,640]{1,0:T(8,128)(2,1)S(1)}, bf16[320,640]{1,0:T(8,128)(2,1)}, u32[]{:S(2)}) copy-start(bf16[320,640]{1,0:T(8,128)(2,1)} %wv_hbm.1) | copy-start | bytes 1228804
  5.5 1.0 %copy-start.4 = (bf16[160,1280]{1,0:T(8,128)(2,1)S(1)}, bf16[160,1280]{1,0:T(8,128)(2,1)}, u32[]{:S(2)}) copy-start(bf16[160,1280]{1,0:T(8,128)(2,1)} %wo_hbm.1) | copy-start | bytes 1228804

commit v2 on v1

v2 whole, which is shorter than its diff:
```python
import jax
import jax.numpy as jnp
from jax import lax
from jax.experimental import pallas as pl
from jax.experimental.pallas import tpu as pltpu
from jax.sharding import PartitionSpec as P

MESH = pl.DeviceIdType.MESH
BF = jnp.bfloat16
F32 = jnp.float32

RING = 8
C = 1280
INNER = 640
FRAMES = 16
PLACES = 24
ROWS = FRAMES * PLACES
HALO = 4
PAIRS = 5
SCALE = 0.125
LOW = -1e30
GROUP = 16
WIDE = INNER + 128


def iota(shape, dim):
    return lax.broadcasted_iota(jnp.int32, shape, dim)


def onehot(mask):
    return jnp.where(mask, 1.0, 0.0).astype(BF)


def dot(a, b):
    return jnp.dot(a, b, preferred_element_type=F32)


def dot_t(a, b):
    return lax.dot_general(a, b, (((1,), (1,)), ((), ())), preferred_element_type=F32)


def rem(value, size):
    return lax.rem(value, jnp.int32(size))


def kernel(
    tok_hbm, wq_hbm, wk_hbm, wv_hbm, wo_hbm, halo_s, gf_s, out_ref,
    tok, xt, htok, xht, wq, wk, wv, wo, q_own, qz, qy, k_own, v_own, k_mar, v_mar, k_pool, v_pool,
    mine, rz, ry, poolz, pooly, oz, oy, og, near_o, near_l, att,
    loc_sem, w_send, w_recv, h_send, h_recv, m_send, m_recv, r_send, r_recv, q_send, q_recv, o_send, o_recv,
):
    c = lax.axis_index("clip")
    s = lax.axis_index("space")
    z, xh, y = lax.div(c, jnp.int32(16)), rem(lax.div(c, jnp.int32(8)), 2), rem(c, 8)
    xl, core = lax.div(s, jnp.int32(2)), rem(s, 2)
    x = xh * 2 + xl
    spot = xh * 8 + z

    def dev(z_, xh_, y_, s_):
        return (z_ * 16 + xh_ * 8 + y_, s_)

    mate = (c, xl * 2 + 1 - core)
    up = rem(x + 1, 4)
    down = rem(x + 3, 4)
    x_up = dev(z, lax.div(up, jnp.int32(2)), y, rem(up, 2) * 2 + core)
    x_down = dev(z, lax.div(down, jnp.int32(2)), y, rem(down, 2) * 2 + core)
    clip_next = (rem(c + 1, 128), s)
    clip_prev = (rem(c + 127, 128), s)

    def loop(start, stop, act):
        def step(d, carry):
            act(d)
            return carry

        lax.fori_loop(start, stop, step, 0)

    def group_dev(place):
        return dev(rem(place, 8), lax.div(place, jnp.int32(8)), y, s)

    weights = ((wq_hbm, wq), (wk_hbm, wk), (wv_hbm, wv), (wo_hbm, wo))
    tok_in = pltpu.make_async_copy(tok_hbm, tok, loc_sem.at[0])
    tok_in.start()
    barrier = pltpu.get_barrier_semaphore()

    def greet(device):
        pl.semaphore_signal(barrier, inc=1, device_id=device, device_id_type=MESH)

    for device in (mate, x_up, x_down, clip_next, clip_prev):
        greet(device)
    loop(1, GROUP, lambda d: greet(group_dev(rem(spot + d, GROUP))))
    loop(1, RING, lambda d: greet(dev(z, xh, rem(y + d, RING), s)))
    loop(0, RING, lambda d: greet(dev(z, 1 - xh, rem(y + d, RING), s)))

    def shard(i, index, half=None):
        full = weights[i][1]
        rows = full.shape[0] // 4
        if half is None:
            return full.at[pl.ds(pl.multiple_of(index * rows, 16), rows)]
        return full.at[pl.ds(pl.multiple_of(index * rows + half * (rows // 2), 16), rows // 2)]

    w_in = []
    for i in range(4):
        copy = pltpu.make_async_copy(weights[i][0], shard(i, s), loc_sem.at[1 + i])
        copy.start()
        w_in.append(copy)

    def message(part, d):
        if part == 0:
            place = rem(spot + d, GROUP)
            src, dst, device = mine.at[place], rz.at[spot], group_dev(place)
        else:
            place = rem(y + d, RING)
            xh_ = rem(xh + lax.div(d, jnp.int32(8)), 2)
            src, dst, device = mine.at[16 + place], ry.at[xh * 8 + y], dev(z, xh_, place, s)
        return pltpu.make_async_remote_copy(
            src_ref=src, dst_ref=dst, send_sem=m_send.at[part, d], recv_sem=m_recv.at[part, d],
            device_id=device, device_id_type=MESH,
        )

    def each_message(act):
        for part in range(2):
            loop(1, 16, lambda d, part=part: act(message(part, d)))

    def weight_copy(i, kind):
        rows = weights[i][0].shape[0]
        theirs = (1 - xl) * 2 + core
        if kind == 0:
            src, dst, device = weights[i][0].at[pl.ds(0, rows // 2)], shard(i, s, 0), x_up
        elif kind == 1:
            src, dst, device = weights[i][0].at[pl.ds(rows // 2, rows // 2)], shard(i, s, 1), x_down
        elif kind == 2:
            src, dst, device = weights[i][0], shard(i, s), mate
        else:
            src, dst, device = shard(i, theirs, kind - 3), shard(i, theirs, kind - 3), mate
        return pltpu.make_async_remote_copy(
            src_ref=src, dst_ref=dst, send_sem=w_send.at[i, kind], recv_sem=w_recv.at[i, kind],
            device_id=device, device_id_type=MESH,
        )

    def margin_copy(side):
        edge = HALO * PLACES
        src = tok_hbm.at[pl.ds(ROWS - edge, edge)] if side == 0 else tok_hbm.at[pl.ds(0, edge)]
        return pltpu.make_async_remote_copy(
            src_ref=src,
            dst_ref=htok.at[pl.ds(side * edge, edge)],
            send_sem=h_send.at[side],
            recv_sem=h_recv.at[side],
            device_id=clip_next if side == 0 else clip_prev,
            device_id_type=MESH,
        )

    pools = (poolz, pooly)

    def block_copy(part, d):
        if part == 0:
            at, device = y, dev(z, xh, rem(y + d, RING), s)
        else:
            at, device = z, dev(rem(z + d, RING), xh, y, s)
        return pltpu.make_async_remote_copy(
            src_ref=pools[part].at[at], dst_ref=pools[part].at[at],
            send_sem=r_send.at[part, d], recv_sem=r_recv.at[part, d], device_id=device, device_id_type=MESH,
        )

    def each_block(act):
        for part in range(2):
            loop(1, RING, lambda d, part=part: act(block_copy(part, d)))

    def query_copy(part, d):
        if part == 0:
            place = rem(spot + d, GROUP)
            first, dst, device = place, qz.at[spot], group_dev(place)
        else:
            place = rem(y + d, RING)
            first, dst, device = 16 + place, qy.at[y], dev(z, xh, place, s)
        return pltpu.make_async_remote_copy(
            src_ref=q_own.at[pl.ds(pl.multiple_of(first * 16, 16), 16)], dst_ref=dst,
            send_sem=q_send.at[part, d], recv_sem=q_recv.at[part, d], device_id=device, device_id_type=MESH,
        )

    def each_query(act):
        loop(1, GROUP, lambda d: act(query_copy(0, d)))
        loop(1, RING, lambda d: act(query_copy(1, d)))

    def reply_copy(part, d):
        if part == 0:
            place = rem(spot + d, GROUP)
            src, first, device = oz.at[place], spot, group_dev(place)
        else:
            place = rem(y + d, RING)
            src, first, device = oy.at[place], 16 + y, dev(z, xh, place, s)
        return pltpu.make_async_remote_copy(
            src_ref=src, dst_ref=og.at[pl.ds(pl.multiple_of(first * 16, 16), 16)],
            send_sem=o_send.at[part, d], recv_sem=o_recv.at[part, d], device_id=device, device_id_type=MESH,
        )

    def each_reply(part, act):
        loop(1, (GROUP, RING)[part], lambda d: act(reply_copy(part, d)))

    pl.semaphore_wait(barrier, 15 + 7 + 8 + 5)
    for kind in range(3):
        weight_copy(0, kind).start()

    tok_in.wait()
    frame = gf_s[0]
    pick = onehot(iota((PLACES, ROWS), 1) == iota((PLACES, ROWS), 0) + frame * PLACES)
    picked = dot(pick, tok[...]).astype(BF)
    shape = (PLACES * 16, PLACES)
    match = iota(shape, 1) == (iota(shape, 0) >> 4)
    row = iota(shape, 0) & 15
    total = jnp.zeros((PLACES * 16, 128), F32)
    for j in range(10):
        total = total + dot(onehot(match & (row == j)), picked[:, 128 * j : 128 * j + 128])
    mine[...] = total.astype(BF).reshape(PLACES, 16, 128)
    each_message(lambda copy: copy.start())

    for side in range(2):
        margin_copy(side).start()
    for i in range(1, 4):
        for kind in range(3):
            weight_copy(i, kind).start()

    shape = (ROWS, ROWS)
    turn = onehot(iota(shape, 1) == (iota(shape, 0) & 15) * PLACES + (iota(shape, 0) >> 4))
    xt[...] = dot(turn, tok[...]).astype(BF)

    rz[spot] = mine[spot]
    ry[xh * 8 + y] = mine[16 + y]
    each_message(lambda copy: copy.wait_recv())
    r, col = iota((16, 256), 0), iota((16, 256), 1)
    for part, land, at in ((0, rz, y), (1, ry, z)):
        rows = land[...].reshape(256, 128)
        for j in range(10):
            choose = onehot((r == (col >> 4)) & ((col & 15) == j))
            pools[part][at, :, 128 * j : 128 * j + 128] = dot(choose, rows).astype(BF)
    each_block(lambda copy: copy.start())

    def pass_on(i):
        for half in range(2):
            weight_copy(i, half).wait_recv()
            weight_copy(i, 3 + half).start()

    def whole(i):
        w_in[i].wait()
        for kind in range(2, 5):
            weight_copy(i, kind).wait_recv()

    pass_on(0)
    whole(0)
    q_own[...] = (dot(xt[...], wq[...]) * SCALE).astype(BF)
    each_query(lambda copy: copy.start())
    qz[spot] = q_own[pl.ds(pl.multiple_of(spot * 16, 16), 16)]
    qy[y] = q_own[pl.ds(pl.multiple_of(256 + y * 16, 16), 16)]

    pass_on(1)
    whole(1)
    k_own[...] = dot(xt[...], wk[...]).astype(BF)
    each_block(lambda copy: copy.wait_recv())
    pass_on(2)
    for part in range(2):
        k_pool[part] = dot(pools[part][...].reshape(RING * 16, C), wk[...]).astype(BF)
    whole(2)
    for part in range(2):
        v_pool[part] = dot(pools[part][...].reshape(RING * 16, C), wv[...]).astype(BF)

    lane = iota((128, 128), 1)
    left = lane < 64
    left_b = onehot(iota((1, 128), 1) < 64)
    right_b = onehot(iota((1, 128), 1) >= 64)
    each_query(lambda copy: copy.wait_recv())

    def far(part, queries, out, start):
        logs = jnp.zeros((128, 128), F32)
        for pair in range(PAIRS):
            lanes = slice(128 * pair, 128 * pair + 128)
            q = queries[pl.ds(start, 8), :, lanes].reshape(128, 128)
            keys = k_pool[part, :, lanes]
            values = v_pool[part, :, lanes]
            scores = dot_t(q, jnp.concatenate([keys * left_b, keys * right_b], axis=0))
            s0, s1 = scores[:, :128], scores[:, 128:]
            m0 = jnp.max(s0, axis=1, keepdims=True)
            m1 = jnp.max(s1, axis=1, keepdims=True)
            e0 = jnp.exp(s0 - m0)
            e1 = jnp.exp(s1 - m1)
            l0 = jnp.sum(e0, axis=1, keepdims=True)
            l1 = jnp.sum(e1, axis=1, keepdims=True)
            mixed = dot(
                jnp.concatenate([e0.astype(BF), e1.astype(BF)], axis=1),
                jnp.concatenate([values * left_b, values * right_b], axis=0),
            )
            mixed = mixed * jnp.where(left, 1.0 / l0, 1.0 / l1)
            out[pl.ds(start, 8), :, lanes] = mixed.astype(BF).reshape(RING, 16, 128)
            logs = jnp.where(lane == 2 * pair, m0 + jnp.log(l0), logs)
            logs = jnp.where(lane == 2 * pair + 1, m1 + jnp.log(l1), logs)
        high = logs.astype(BF).astype(F32)
        middle = (logs - high).astype(BF).astype(F32)
        low = (logs - high - middle).astype(BF).astype(F32)
        packed = high + pltpu.roll(middle, 16, 1) + pltpu.roll(low, 32, 1)
        out[pl.ds(start, 8), :, INNER:] = packed.astype(BF).reshape(RING, 16, 128)

    for half in range(2):
        far(0, qz, oz, 8 * half)
    each_reply(0, lambda copy: copy.start())
    far(1, qy, oy, 0)
    each_reply(1, lambda copy: copy.start())
    og[pl.ds(pl.multiple_of(spot * 16, 16), 16)] = oz[spot]
    og[pl.ds(pl.multiple_of(256 + y * 16, 16), 16)] = oy[y]

    pass_on(3)

    for side in range(2):
        margin_copy(side).wait_recv()
    edge = 2 * HALO * PLACES
    shape = (edge, edge)
    turn = onehot(iota(shape, 1) == (iota(shape, 0) & 7) * PLACES + (iota(shape, 0) >> 3))
    xht[...] = dot(turn, htok[...]).astype(BF)
    k_mar[...] = dot(xht[...], wk[...]).astype(BF)
    v_mar[...] = dot(xht[...], wv[...]).astype(BF)
    v_own[...] = dot(xt[...], wv[...]).astype(BF)

    row8 = iota((128, 128), 0) >> 4
    own_bias = jnp.where(row8 == (lane >> 4), 0.0, LOW)
    half = lane & 63
    slot = half & 7
    reach = halo_s[0]
    before = (slot < HALO) & (c > 0) & (HALO - slot <= reach)
    after = (slot >= HALO) & (c < 127) & (slot - HALO + 1 <= reach)
    mar_bias = jnp.where((row8 == (half >> 3)) & (before | after), 0.0, LOW)
    for g in range(3):
        rows = slice(128 * g, 128 * g + 128)
        edges = slice(64 * g, 64 * g + 64)
        logs = jnp.zeros((128, 128), F32)
        for pair in range(PAIRS):
            lanes = slice(128 * pair, 128 * pair + 128)
            q = q_own[rows, lanes]
            ko, vo, km, vm = k_own[rows, lanes], v_own[rows, lanes], k_mar[edges, lanes], v_mar[edges, lanes]
            scores = dot_t(q, jnp.concatenate([ko * left_b, ko * right_b, km * left_b, km * right_b], axis=0))
            s0 = scores[:, :128] + own_bias
            s1 = scores[:, 128:256] + own_bias
            sm = scores[:, 256:] + mar_bias
            m0 = jnp.max(jnp.maximum(s0, jnp.where(left, sm, LOW)), axis=1, keepdims=True)
            m1 = jnp.max(jnp.maximum(s1, jnp.where(left, LOW, sm)), axis=1, keepdims=True)
            e0 = jnp.exp(s0 - m0)
            e1 = jnp.exp(s1 - m1)
            em = jnp.exp(sm - jnp.where(left, m0, m1))
            l0 = jnp.sum(e0 + jnp.where(left, em, 0.0), axis=1, keepdims=True)
            l1 = jnp.sum(e1 + jnp.where(left, 0.0, em), axis=1, keepdims=True)
            mixed = dot(
                jnp.concatenate([e0.astype(BF), e1.astype(BF), em.astype(BF)], axis=1),
                jnp.concatenate([vo * left_b, vo * right_b, vm * left_b, vm * right_b], axis=0),
            )
            near_o[rows, lanes] = mixed * jnp.where(left, 1.0 / l0, 1.0 / l1)
            logs = jnp.where(lane == 2 * pair, m0 + jnp.log(l0), logs)
            logs = jnp.where(lane == 2 * pair + 1, m1 + jnp.log(l1), logs)
        near_l[rows, :] = logs

    for part in range(2):
        each_reply(part, lambda copy: copy.wait_recv())
    r128, c128 = iota((128, 128), 0), iota((128, 128), 1)
    gather_logs = onehot(((r128 & 15) == c128) & (r128 < 48) & (c128 < 10))
    expand = onehot(iota((128, INNER), 0) == (iota((128, INNER), 1) >> 6))
    for g in range(3):
        rows = slice(128 * g, 128 * g + 128)
        far_l = dot(og[rows, INNER:], gather_logs)
        share = 1.0 / (1.0 + jnp.exp(near_l[rows, :] - far_l))
        high = share.astype(BF)
        rest = (share - high.astype(F32)).astype(BF)
        wide = dot(high, expand) + dot(rest, expand)
        near = near_o[rows, :]
        att[rows, :] = (near + wide * (og[rows, :INNER].astype(F32) - near)).astype(BF)
    shape = (ROWS, ROWS)
    turn = onehot(iota(shape, 0) == (iota(shape, 1) & 15) * PLACES + (iota(shape, 1) >> 4))
    ordered = dot(turn, att[...]).astype(BF)
    whole(3)
    out_ref[...] = dot(ordered, wo[...]).astype(BF)

    each_message(lambda copy: copy.wait_send())
    for i in range(4):
        for kind in range(5):
            weight_copy(i, kind).wait_send()
    for side in range(2):
        margin_copy(side).wait_send()
    each_block(lambda copy: copy.wait_send())
    each_query(lambda copy: copy.wait_send())
    for part in range(2):
        each_reply(part, lambda copy: copy.wait_send())


def body(tokens, w_query, w_key, w_value, w_out, halo_width, global_frame):
    rows = tokens.reshape(ROWS, C)
    any_spec = pl.BlockSpec(memory_space=pl.ANY)
    smem = pl.BlockSpec(memory_space=pltpu.SMEM)
    v = pltpu.VMEM
    dma = pltpu.SemaphoreType.DMA
    edge = 2 * HALO * PLACES
    out = pl.pallas_call(
        kernel,
        out_shape=jax.ShapeDtypeStruct((ROWS, C), BF),
        in_specs=[any_spec] * 5 + [smem] * 2,
        out_specs=pl.BlockSpec(memory_space=pltpu.VMEM),
        scratch_shapes=[
            v((ROWS, C), BF), v((ROWS, C), BF), v((edge, C), BF), v((edge, C), BF),
            v((C, INNER), BF), v((C, INNER), BF), v((C, INNER), BF), v((INNER, C), BF),
            v((ROWS, INNER), BF), v((GROUP, 16, INNER), BF), v((RING, 16, INNER), BF),
            v((ROWS, INNER), BF), v((ROWS, INNER), BF), v((edge, INNER), BF), v((edge, INNER), BF),
            v((2, 128, INNER), BF), v((2, 128, INNER), BF),
            v((PLACES, 16, 128), BF), v((GROUP, 16, 128), BF), v((GROUP, 16, 128), BF),
            v((RING, 16, C), BF), v((RING, 16, C), BF),
            v((GROUP, 16, WIDE), BF), v((RING, 16, WIDE), BF), v((ROWS, WIDE), BF),
            v((ROWS, INNER), F32), v((ROWS, 128), F32), v((ROWS, INNER), BF),
            dma((5,)), dma((4, 5)), dma((4, 5)), dma((2,)), dma((2,)), dma((2, 16)), dma((2, 16)),
            dma((2, 8)), dma((2, 8)), dma((2, 16)), dma((2, 16)), dma((2, 16)), dma((2, 16)),
        ],
        compiler_params=pltpu.CompilerParams(
            collective_id=0, has_side_effects=True, vmem_limit_bytes=60 * 1024 * 1024
        ),
    )(rows, w_query, w_key, w_value, w_out, halo_width, global_frame)
    return out.reshape(FRAMES, PLACES, C)


def solution(mesh):
    return jax.shard_map(
        body,
        mesh=mesh,
        in_specs=(
            P("clip", "space", None),
            P("space", None),
            P("space", None),
            P("space", None),
            P("space", None),
            P("clip"),
            P("clip"),
        ),
        out_specs=P("clip", "space", None),
        check_vma=False,
    )
```

time: 77.5 us -> 67.4 us (0.87)
  Pallas kernels: 69.7 us -> 63.7 us
  local copies, waits for them, and re-layouts: 6.15 us -> 2.21 us
    pallas_call x1, Pallas kernels: 69.7 us -> 63.7 us  [body(): pl.pallas_call(kernel, out_shape=jax.ShapeDtypeStruct((ROWS, C), BF), in_...]
    unnamed x11 -> x1, local copies, waits for them, and re-layouts: 6.15 us -> 2.21 us
where the time goes in v2:
time: 67.4 us; the launch traced here: 67.2 us
  Pallas kernels  63.7 us (95%)
  local copies, waits for them, and re-layouts  2.21 us (3%)
  between operations  1.3 us (2%)
    pallas_call x1, Pallas kernels, body(): pl.pallas_call(kernel, out_shape=jax.ShapeDtypeStruct((ROWS, C), BF), in_...  63.7 us
    unnamed x1, local copies, waits for them, and re-layouts  2.21 us

profile of v2, /device:TPU:1, one launch (start us, length us, event | category | flops | bytes accessed | tf_op | source)
XLA Modules:
  0.0 67.2 jit_solution(7331052277955434480)
XLA Ops:
  1.3 63.7 %shard_map.73 = bf16[384,1280]{1,0:T(8,128)(2,1)} custom-call(bf16[384,1280]{1,0:T(8,128)(2,1)} %bitcast.3, bf16[320,640]{1,0:T(8,128)(2,1)} %wq_hbm.1, bf16[320,640]{1,0:T(8,128)(2,1)} %wk_hbm.1, bf16[320,640]{1,0:T(8,128)(2,1)} %wv_hbm.1, bf16[160,1280]{1,0:T(8,128)(2,1)} %wo_hbm.1, s32[1]{0:T(128)S(6)} %copy.9.halo_s, s32[1]{0:T(128)S(6)} %copy.10.gf_s), custom_call_target="tpu_custom_call" | custom-call | tf_op jit(solution)/shard_map/pallas_call | solution.py:395
  65.0 2.2 %copy.11 = bf16[16,24,1280]{2,1,0:T(8,128)(2,1)} copy(bf16[16,24,1280]{2,1,0:T(8,128)(2,1)} %bitcast.2) | data formatting | bytes 1966080

commit v3 on v2

--- a/solution.py
+++ b/solution.py
@@ -19,7 +19,7 @@
 PAIRS = 5
 SCALE = 0.125
 LOW = -1e30
-GROUP = 16
+SPOTS = ((0, 0), (0, 1), (1, 0))
 WIDE = INNER + 128
 
 
@@ -46,7 +46,7 @@
 def kernel(
     tok_hbm, wq_hbm, wk_hbm, wv_hbm, wo_hbm, halo_s, gf_s, out_ref,
     tok, xt, htok, xht, wq, wk, wv, wo, q_own, qz, qy, k_own, v_own, k_mar, v_mar, k_pool, v_pool,
-    mine, rz, ry, poolz, pooly, oz, oy, og, near_o, near_l, att,
+    mine, rz, ry, pool, answers, og, near_o, near_l, att,
     loc_sem, w_send, w_recv, h_send, h_recv, m_send, m_recv, r_send, r_recv, q_send, q_recv, o_send, o_recv,
 ):
     c = lax.axis_index("clip")
@@ -54,7 +54,6 @@
     z, xh, y = lax.div(c, jnp.int32(16)), rem(lax.div(c, jnp.int32(8)), 2), rem(c, 8)
     xl, core = lax.div(s, jnp.int32(2)), rem(s, 2)
     x = xh * 2 + xl
-    spot = xh * 8 + z
 
     def dev(z_, xh_, y_, s_):
         return (z_ * 16 + xh_ * 8 + y_, s_)
@@ -74,8 +73,9 @@
 
         lax.fori_loop(start, stop, step, 0)
 
-    def group_dev(place):
-        return dev(rem(place, 8), lax.div(place, jnp.int32(8)), y, s)
+    def ring_dev(part, place, other=0):
+        xh_ = rem(xh + other, 2)
+        return dev(place, xh_, y, s) if part == 0 else dev(z, xh_, place, s)
 
     weights = ((wq_hbm, wq), (wk_hbm, wk), (wv_hbm, wv), (wo_hbm, wo))
     tok_in = pltpu.make_async_copy(tok_hbm, tok, loc_sem.at[0])
@@ -87,9 +87,8 @@
 
     for device in (mate, x_up, x_down, clip_next, clip_prev):
         greet(device)
-    loop(1, GROUP, lambda d: greet(group_dev(rem(spot + d, GROUP))))
-    loop(1, RING, lambda d: greet(dev(z, xh, rem(y + d, RING), s)))
-    loop(0, RING, lambda d: greet(dev(z, 1 - xh, rem(y + d, RING), s)))
+    for part in range(2):
+        loop(1, 16, lambda d, part=part: greet(ring_dev(part, rem((z, y)[part] + d, RING), lax.div(d, jnp.int32(8)))))
 
     def shard(i, index, half=None):
         full = weights[i][1]
@@ -105,16 +104,14 @@
         w_in.append(copy)
 
     def message(part, d):
+        place = rem((z, y)[part] + d, RING)
         if part == 0:
-            place = rem(spot + d, GROUP)
-            src, dst, device = mine.at[place], rz.at[spot], group_dev(place)
+            src, dst = mine.at[pl.ds(2 * place, 2)], rz.at[xh * 8 + z]
         else:
-            place = rem(y + d, RING)
-            xh_ = rem(xh + lax.div(d, jnp.int32(8)), 2)
-            src, dst, device = mine.at[16 + place], ry.at[xh * 8 + y], dev(z, xh_, place, s)
+            src, dst = mine.at[16 + place], ry.at[xh * 8 + y]
         return pltpu.make_async_remote_copy(
             src_ref=src, dst_ref=dst, send_sem=m_send.at[part, d], recv_sem=m_recv.at[part, d],
-            device_id=device, device_id_type=MESH,
+            device_id=ring_dev(part, place, lax.div(d, jnp.int32(8))), device_id_type=MESH,
         )
 
     def each_message(act):
@@ -149,73 +146,74 @@
             device_id_type=MESH,
         )
 
-    pools = (poolz, pooly)
-
-    def block_copy(part, d):
+    def block_copy(part, k):
+        here = (y, z)[part]
+        hop = (1, 2, 7, 6, 1, 2, 7, 6)[k]
+        origin = here if k < 4 else rem(here + (6 if k < 6 else 2), RING)
+        place = rem(here + hop, RING)
+        device = dev(z, xh, place, s) if part == 0 else dev(place, xh, y, s)
         if part == 0:
-            at, device = y, dev(z, xh, rem(y + d, RING), s)
+            block = pool.at[origin, k // 7] if k in (5, 7) else pool.at[origin, pl.ds(0, 2)]
+        elif k in (5, 7):
+            block = pool.at[origin, 2, :, pl.ds(k // 7 * (C // 2), C // 2)]
         else:
-            at, device = z, dev(rem(z + d, RING), xh, y, s)
-        return pltpu.make_async_remote_copy(
-            src_ref=pools[part].at[at], dst_ref=pools[part].at[at],
-            send_sem=r_send.at[part, d], recv_sem=r_recv.at[part, d], device_id=device, device_id_type=MESH,
-        )
-
-    def each_block(act):
+            block = pool.at[origin, 2]
+        return pltpu.make_async_remote_copy(
+            src_ref=block, dst_ref=block,
+            send_sem=r_send.at[part, k], recv_sem=r_recv.at[part, k], device_id=device, device_id_type=MESH,
+        )
+
+    def each_block(ks, act):
         for part in range(2):
-            loop(1, RING, lambda d, part=part: act(block_copy(part, d)))
+            for k in ks:
+                act(block_copy(part, k))
 
     def query_copy(part, d):
+        place = rem((z, y)[part] + d, RING)
         if part == 0:
-            place = rem(spot + d, GROUP)
-            first, dst, device = place, qz.at[spot], group_dev(place)
+            src, dst = q_own.at[pl.ds(pl.multiple_of(place * 32, 16), 32)], qz.at[z]
         else:
-            place = rem(y + d, RING)
-            first, dst, device = 16 + place, qy.at[y], dev(z, xh, place, s)
-        return pltpu.make_async_remote_copy(
-            src_ref=q_own.at[pl.ds(pl.multiple_of(first * 16, 16), 16)], dst_ref=dst,
-            send_sem=q_send.at[part, d], recv_sem=q_recv.at[part, d], device_id=device, device_id_type=MESH,
+            src, dst = q_own.at[pl.ds(pl.multiple_of(256 + place * 16, 16), 16)], qy.at[y]
+        return pltpu.make_async_remote_copy(
+            src_ref=src, dst_ref=dst, send_sem=q_send.at[part, d], recv_sem=q_recv.at[part, d],
+            device_id=ring_dev(part, place), device_id_type=MESH,
         )
 
     def each_query(act):
-        loop(1, GROUP, lambda d: act(query_copy(0, d)))
-        loop(1, RING, lambda d: act(query_copy(1, d)))
-
-    def reply_copy(part, d):
-        if part == 0:
-            place = rem(spot + d, GROUP)
-            src, first, device = oz.at[place], spot, group_dev(place)
-        else:
-            place = rem(y + d, RING)
-            src, first, device = oy.at[place], 16 + y, dev(z, xh, place, s)
-        return pltpu.make_async_remote_copy(
-            src_ref=src, dst_ref=og.at[pl.ds(pl.multiple_of(first * 16, 16), 16)],
-            send_sem=o_send.at[part, d], recv_sem=o_recv.at[part, d], device_id=device, device_id_type=MESH,
-        )
-
-    def each_reply(part, act):
-        loop(1, (GROUP, RING)[part], lambda d: act(reply_copy(part, d)))
-
-    pl.semaphore_wait(barrier, 15 + 7 + 8 + 5)
+        for part in range(2):
+            loop(1, RING, lambda d, part=part: act(query_copy(part, d)))
+
+    def answer_rows(k):
+        part, p = SPOTS[k]
+        return pl.ds(pl.multiple_of((2 * z + p) * 16 if part == 0 else (16 + y) * 16, 16), 16)
+
+    def reply_copy(k, d):
+        part = SPOTS[k][0]
+        place = rem((z, y)[part] + d, RING)
+        return pltpu.make_async_remote_copy(
+            src_ref=answers.at[k, place], dst_ref=og.at[answer_rows(k)],
+            send_sem=o_send.at[k, d], recv_sem=o_recv.at[k, d], device_id=ring_dev(part, place), device_id_type=MESH,
+        )
+
+    def each_reply(k, act):
+        loop(1, RING, lambda d: act(reply_copy(k, d)))
+
+    pl.semaphore_wait(barrier, 15 + 15 + 5)
     for kind in range(3):
         weight_copy(0, kind).start()
 
     tok_in.wait()
     frame = gf_s[0]
-    pick = onehot(iota((PLACES, ROWS), 1) == iota((PLACES, ROWS), 0) + frame * PLACES)
-    picked = dot(pick, tok[...]).astype(BF)
-    shape = (PLACES * 16, PLACES)
-    match = iota(shape, 1) == (iota(shape, 0) >> 4)
-    row = iota(shape, 0) & 15
-    total = jnp.zeros((PLACES * 16, 128), F32)
+    shape = (ROWS, ROWS)
+    spread = dot(onehot(iota(shape, 1) == frame * PLACES + (iota(shape, 0) >> 4)), tok[...])
+    row = iota((ROWS, 128), 0) & 15
+    total = jnp.zeros((ROWS, 128), F32)
     for j in range(10):
-        total = total + dot(onehot(match & (row == j)), picked[:, 128 * j : 128 * j + 128])
+        total = jnp.where(row == j, spread[:, 128 * j : 128 * j + 128], total)
     mine[...] = total.astype(BF).reshape(PLACES, 16, 128)
     each_message(lambda copy: copy.start())
 
-    for side in range(2):
-        margin_copy(side).start()
-    for i in range(1, 4):
+    for i in range(1, 3):
         for kind in range(3):
             weight_copy(i, kind).start()
 
@@ -223,16 +221,17 @@
     turn = onehot(iota(shape, 1) == (iota(shape, 0) & 15) * PLACES + (iota(shape, 0) >> 4))
     xt[...] = dot(turn, tok[...]).astype(BF)
 
-    rz[spot] = mine[spot]
+    rz[xh * 8 + z] = mine[pl.ds(2 * z, 2)]
     ry[xh * 8 + y] = mine[16 + y]
     each_message(lambda copy: copy.wait_recv())
-    r, col = iota((16, 256), 0), iota((16, 256), 1)
-    for part, land, at in ((0, rz, y), (1, ry, z)):
-        rows = land[...].reshape(256, 128)
+    r, col = iota((160, 256), 0), iota((160, 256), 1)
+    choose = onehot(((r & 15) == (col >> 4)) & ((col & 15) == (r >> 4)))
+    for k, (part, p) in enumerate(SPOTS):
+        rows = (rz[:, p] if part == 0 else ry[...]).reshape(256, 128)
+        block = dot(choose, rows).astype(BF)
         for j in range(10):
-            choose = onehot((r == (col >> 4)) & ((col & 15) == j))
-            pools[part][at, :, 128 * j : 128 * j + 128] = dot(choose, rows).astype(BF)
-    each_block(lambda copy: copy.start())
+            pool[(y, z)[part], k, :, 128 * j : 128 * j + 128] = block[16 * j : 16 * j + 16]
+    each_block((1, 3, 0, 2), lambda copy: copy.start())
 
     def pass_on(i):
         for half in range(2):
@@ -248,19 +247,23 @@
     whole(0)
     q_own[...] = (dot(xt[...], wq[...]) * SCALE).astype(BF)
     each_query(lambda copy: copy.start())
-    qz[spot] = q_own[pl.ds(pl.multiple_of(spot * 16, 16), 16)]
+    qz[z] = q_own[pl.ds(pl.multiple_of(z * 32, 16), 32)]
     qy[y] = q_own[pl.ds(pl.multiple_of(256 + y * 16, 16), 16)]
+    each_block((1, 3), lambda copy: copy.wait_recv())
+    each_block((4, 5, 6, 7), lambda copy: copy.start())
 
     pass_on(1)
+    for kind in range(3):
+        weight_copy(3, kind).start()
     whole(1)
     k_own[...] = dot(xt[...], wk[...]).astype(BF)
-    each_block(lambda copy: copy.wait_recv())
     pass_on(2)
-    for part in range(2):
-        k_pool[part] = dot(pools[part][...].reshape(RING * 16, C), wk[...]).astype(BF)
+    for side in range(2):
+        margin_copy(side).start()
+    each_block((0, 2, 4, 5, 6, 7), lambda copy: copy.wait_recv())
+    k_pool[...] = dot(pool[...].reshape(ROWS, C), wk[...]).astype(BF).reshape(RING, 3, 16, INNER)
     whole(2)
-    for part in range(2):
-        v_pool[part] = dot(pools[part][...].reshape(RING * 16, C), wv[...]).astype(BF)
+    v_pool[...] = dot(pool[...].reshape(ROWS, C), wv[...]).astype(BF).reshape(RING, 3, 16, INNER)
 
     lane = iota((128, 128), 1)
     left = lane < 64
@@ -268,13 +271,14 @@
     right_b = onehot(iota((1, 128), 1) >= 64)
     each_query(lambda copy: copy.wait_recv())
 
-    def far(part, queries, out, start):
+    for k, (part, p) in enumerate(SPOTS):
+        queries = (qz, qy)[part]
         logs = jnp.zeros((128, 128), F32)
         for pair in range(PAIRS):
             lanes = slice(128 * pair, 128 * pair + 128)
-            q = queries[pl.ds(start, 8), :, lanes].reshape(128, 128)
-            keys = k_pool[part, :, lanes]
-            values = v_pool[part, :, lanes]
+            q = queries[:, 16 * p : 16 * p + 16, lanes].reshape(128, 128)
+            keys = k_pool[:, k, :, lanes].reshape(128, 128)
+            values = v_pool[:, k, :, lanes].reshape(128, 128)
             scores = dot_t(q, jnp.concatenate([keys * left_b, keys * right_b], axis=0))
             s0, s1 = scores[:, :128], scores[:, 128:]
             m0 = jnp.max(s0, axis=1, keepdims=True)
@@ -288,23 +292,18 @@
                 jnp.concatenate([values * left_b, values * right_b], axis=0),
             )
             mixed = mixed * jnp.where(left, 1.0 / l0, 1.0 / l1)
-            out[pl.ds(start, 8), :, lanes] = mixed.astype(BF).reshape(RING, 16, 128)
+            answers[k, :, :, lanes] = mixed.astype(BF).reshape(RING, 16, 128)
             logs = jnp.where(lane == 2 * pair, m0 + jnp.log(l0), logs)
             logs = jnp.where(lane == 2 * pair + 1, m1 + jnp.log(l1), logs)
         high = logs.astype(BF).astype(F32)
         middle = (logs - high).astype(BF).astype(F32)
         low = (logs - high - middle).astype(BF).astype(F32)
         packed = high + pltpu.roll(middle, 16, 1) + pltpu.roll(low, 32, 1)
-        out[pl.ds(start, 8), :, INNER:] = packed.astype(BF).reshape(RING, 16, 128)
-
-    for half in range(2):
-        far(0, qz, oz, 8 * half)
-    each_reply(0, lambda copy: copy.start())
-    far(1, qy, oy, 0)
-    each_reply(1, lambda copy: copy.start())
-    og[pl.ds(pl.multiple_of(spot * 16, 16), 16)] = oz[spot]
-    og[pl.ds(pl.multiple_of(256 + y * 16, 16), 16)] = oy[y]
-
+        answers[k, :, :, INNER:] = packed.astype(BF).reshape(RING, 16, 128)
+        each_reply(k, lambda copy: copy.start())
+        og[answer_rows(k)] = answers[k, (z, y)[part]]
+
+    v_own[...] = dot(xt[...], wv[...]).astype(BF)
     pass_on(3)
 
     for side in range(2):
@@ -315,7 +314,6 @@
     xht[...] = dot(turn, htok[...]).astype(BF)
     k_mar[...] = dot(xht[...], wk[...]).astype(BF)
     v_mar[...] = dot(xht[...], wv[...]).astype(BF)
-    v_own[...] = dot(xt[...], wv[...]).astype(BF)
 
     row8 = iota((128, 128), 0) >> 4
     own_bias = jnp.where(row8 == (lane >> 4), 0.0, LOW)
@@ -353,8 +351,17 @@
             logs = jnp.where(lane == 2 * pair + 1, m1 + jnp.log(l1), logs)
         near_l[rows, :] = logs
 
-    for part in range(2):
-        each_reply(part, lambda copy: copy.wait_recv())
+    each_message(lambda copy: copy.wait_send())
+    for i in range(3):
+        for kind in range(5):
+            weight_copy(i, kind).wait_send()
+    for side in range(2):
+        margin_copy(side).wait_send()
+    each_block(range(8), lambda copy: copy.wait_send())
+    each_query(lambda copy: copy.wait_send())
+
+    for k in range(3):
+        each_reply(k, lambda copy: copy.wait_recv())
     r128, c128 = iota((128, 128), 0), iota((128, 128), 1)
     gather_logs = onehot(((r128 & 15) == c128) & (r128 < 48) & (c128 < 10))
     expand = onehot(iota((128, INNER), 0) == (iota((128, INNER), 1) >> 6))
@@ -373,16 +380,10 @@
     whole(3)
     out_ref[...] = dot(ordered, wo[...]).astype(BF)
 
-    each_message(lambda copy: copy.wait_send())
-    for i in range(4):
-        for kind in range(5):
-            weight_copy(i, kind).wait_send()
-    for side in range(2):
-        margin_copy(side).wait_send()
-    each_block(lambda copy: copy.wait_send())
-    each_query(lambda copy: copy.wait_send())
-    for part in range(2):
-        each_reply(part, lambda copy: copy.wait_send())
+    for kind in range(5):
+        weight_copy(3, kind).wait_send()
+    for k in range(3):
+        each_reply(k, lambda copy: copy.wait_send())
 
 
 def body(tokens, w_query, w_key, w_value, w_out, halo_width, global_frame):
@@ -400,15 +401,15 @@
         scratch_shapes=[
             v((ROWS, C), BF), v((ROWS, C), BF), v((edge, C), BF), v((edge, C), BF),
             v((C, INNER), BF), v((C, INNER), BF), v((C, INNER), BF), v((INNER, C), BF),
-            v((ROWS, INNER), BF), v((GROUP, 16, INNER), BF), v((RING, 16, INNER), BF),
+            v((ROWS, INNER), BF), v((RING, 32, INNER), BF), v((RING, 16, INNER), BF),
             v((ROWS, INNER), BF), v((ROWS, INNER), BF), v((edge, INNER), BF), v((edge, INNER), BF),
-            v((2, 128, INNER), BF), v((2, 128, INNER), BF),
-            v((PLACES, 16, 128), BF), v((GROUP, 16, 128), BF), v((GROUP, 16, 128), BF),
-            v((RING, 16, C), BF), v((RING, 16, C), BF),
-            v((GROUP, 16, WIDE), BF), v((RING, 16, WIDE), BF), v((ROWS, WIDE), BF),
+            v((RING, 3, 16, INNER), BF), v((RING, 3, 16, INNER), BF),
+            v((PLACES, 16, 128), BF), v((16, 2, 16, 128), BF), v((16, 16, 128), BF),
+            v((RING, 3, 16, C), BF),
+            v((3, RING, 16, WIDE), BF), v((ROWS, WIDE), BF),
             v((ROWS, INNER), F32), v((ROWS, 128), F32), v((ROWS, INNER), BF),
             dma((5,)), dma((4, 5)), dma((4, 5)), dma((2,)), dma((2,)), dma((2, 16)), dma((2, 16)),
-            dma((2, 8)), dma((2, 8)), dma((2, 16)), dma((2, 16)), dma((2, 16)), dma((2, 16)),
+            dma((2, 8)), dma((2, 8)), dma((2, 8)), dma((2, 8)), dma((3, 8)), dma((3, 8)),
         ],
         compiler_params=pltpu.CompilerParams(
             collective_id=0, has_side_effects=True, vmem_limit_bytes=60 * 1024 * 1024

time: 67.4 us -> 65 us (0.964)
  the two profiles are of different devices: /device:TPU:1 before, /device:TPU:5 now
where the time goes in v3:
time: 65 us; the launch traced here: 64.9 us
  Pallas kernels  61.3 us (94%)
  local copies, waits for them, and re-layouts  2.21 us (3%)
  between operations  1.3 us (2%)
    pallas_call x1, Pallas kernels, body(): pl.pallas_call(kernel, out_shape=jax.ShapeDtypeStruct((ROWS, C), BF), in_...  61.3 us
    unnamed x1, local copies, waits for them, and re-layouts  2.21 us

profile of v3, /device:TPU:5, one launch (start us, length us, event | category | flops | bytes accessed | tf_op | source)
XLA Modules:
  0.0 64.9 jit_solution(9635996083307821659)
XLA Ops:
  1.3 61.3 %shard_map.73 = bf16[384,1280]{1,0:T(8,128)(2,1)} custom-call(bf16[384,1280]{1,0:T(8,128)(2,1)} %bitcast.3, bf16[320,640]{1,0:T(8,128)(2,1)} %wq_hbm.1, bf16[320,640]{1,0:T(8,128)(2,1)} %wk_hbm.1, bf16[320,640]{1,0:T(8,128)(2,1)} %wv_hbm.1, bf16[160,1280]{1,0:T(8,128)(2,1)} %wo_hbm.1, s32[1]{0:T(128)S(6)} %copy.9.halo_s, s32[1]{0:T(128)S(6)} %copy.10.gf_s), custom_call_target="tpu_custom_call" | custom-call | tf_op jit(solution)/shard_map/pallas_call | solution.py:396
  62.6 2.2 %copy.11 = bf16[16,24,1280]{2,1,0:T(8,128)(2,1)} copy(bf16[16,24,1280]{2,1,0:T(8,128)(2,1)} %bitcast.2) | data formatting | bytes 1966080

commit v4 on v3

--- a/solution.py
+++ b/solution.py
@@ -256,10 +256,10 @@
     for kind in range(3):
         weight_copy(3, kind).start()
     whole(1)
+    for side in range(2):
+        margin_copy(side).start()
     k_own[...] = dot(xt[...], wk[...]).astype(BF)
     pass_on(2)
-    for side in range(2):
-        margin_copy(side).start()
     each_block((0, 2, 4, 5, 6, 7), lambda copy: copy.wait_recv())
     k_pool[...] = dot(pool[...].reshape(ROWS, C), wk[...]).astype(BF).reshape(RING, 3, 16, INNER)
     whole(2)
@@ -269,9 +269,11 @@
     left = lane < 64
     left_b = onehot(iota((1, 128), 1) < 64)
     right_b = onehot(iota((1, 128), 1) >= 64)
-    each_query(lambda copy: copy.wait_recv())
-
-    for k, (part, p) in enumerate(SPOTS):
+
+    for k in (2, 0, 1):
+        part, p = SPOTS[k]
+        if k != 1:
+            loop(1, RING, lambda d, part=part: query_copy(part, d).wait_recv())
         queries = (qz, qy)[part]
         logs = jnp.zeros((128, 128), F32)
         for pair in range(PAIRS):
@@ -304,7 +306,6 @@
         og[answer_rows(k)] = answers[k, (z, y)[part]]
 
     v_own[...] = dot(xt[...], wv[...]).astype(BF)
-    pass_on(3)
 
     for side in range(2):
         margin_copy(side).wait_recv()
@@ -351,6 +352,7 @@
             logs = jnp.where(lane == 2 * pair + 1, m1 + jnp.log(l1), logs)
         near_l[rows, :] = logs
 
+    pass_on(3)
     each_message(lambda copy: copy.wait_send())
     for i in range(3):
         for kind in range(5):

time: 65 us -> 65 us (level)
  no operation moved by 1% of the time
where the time goes in v4:
time: 65 us; the launch traced here: 64.8 us
  Pallas kernels  61.3 us (94%)
  local copies, waits for them, and re-layouts  2.21 us (3%)
  between operations  1.3 us (2%)
    pallas_call x1, Pallas kernels, body(): pl.pallas_call(kernel, out_shape=jax.ShapeDtypeStruct((ROWS, C), BF), in_...  61.3 us
    unnamed x1, local copies, waits for them, and re-layouts  2.21 us

profile of v4, /device:TPU:5, one launch (start us, length us, event | category | flops | bytes accessed | tf_op | source)
XLA Modules:
  0.0 64.8 jit_solution(17295107887794822378)
XLA Ops:
  1.3 61.3 %shard_map.73 = bf16[384,1280]{1,0:T(8,128)(2,1)} custom-call(bf16[384,1280]{1,0:T(8,128)(2,1)} %bitcast.3, bf16[320,640]{1,0:T(8,128)(2,1)} %wq_hbm.1, bf16[320,640]{1,0:T(8,128)(2,1)} %wk_hbm.1, bf16[320,640]{1,0:T(8,128)(2,1)} %wv_hbm.1, bf16[160,1280]{1,0:T(8,128)(2,1)} %wo_hbm.1, s32[1]{0:T(128)S(6)} %copy.9.halo_s, s32[1]{0:T(128)S(6)} %copy.10.gf_s), custom_call_target="tpu_custom_call" | custom-call | tf_op jit(solution)/shard_map/pallas_call | solution.py:398
  62.6 2.2 %copy.11 = bf16[16,24,1280]{2,1,0:T(8,128)(2,1)} copy(bf16[16,24,1280]{2,1,0:T(8,128)(2,1)} %bitcast.2) | data formatting | bytes 1966080
